TPU v7x, 32 devices: a whole 2x2x4 slice. The times are simulated.
32 devices in a mesh: src: 8 (over z, y), tgt: 4 (over x, core).
Axes of the slice: x: 2, y: 2, z: 4, core: 2. Of those that a mesh axis runs over, the one named last changes fastest.
Arguments:
- text_emb: bfloat16 [16384, 512], P('src'), may hold values from -32 to 32
- image_emb: bfloat16 [8192, 512], P('tgt'), may hold values from -12 to 12
- log_mass_src: float32 [16384], P('src'), may hold values from -1 to 1
- log_mass_tgt: float32 [8192], P('tgt'), may hold values from -1 to 1
- pair_blocks: int32 [512, 2], P(('src', 'tgt')), may hold values from 0 to 7, as said below
- pair_counts: int32 [32], P(('src', 'tgt')), may hold values from 2 to 16, as said below
Outputs:
- src_map: float32 [16384, 512], P(('src', 'tgt'))
- tgt_map: float32 [8192, 512], P(('tgt', 'src'))
Inputs may be any that keep to these rules, and one draw needn't show every extreme that they name: `pair_blocks`: column 0 is a local text cluster below 8, column 1 a local image cluster below 8. The first pair_counts slots of a device hold distinct pairs; every text cluster and every image cluster lies in some used slot. Unused slots hold valid indices that are ignored. `pair_counts`: at least 8 // 4 used slots on every device; some device uses all 16 in every draw.
All inputs are finite; a program needn't handle non-finite values.
Results may differ from a plain program's by a relative error of at most 0.0028.
Values sent between devices are 32-bit elements; how exact they have to be, the bound alone decides.
A program may use at most 64 MiB of HBM per device.

v0:
```python
import jax
import jax.numpy as jnp
from jax import lax
from jax.sharding import PartitionSpec as P

BLK = 256
ITERS = 3


inv_temp = 0.15
floor_value = -1e30


def merged(part, axis, combine):
    gathered = jax.tree.map(lambda a: lax.all_gather(a, axis), part)

    def take(source):
        return jax.tree.map(lambda a: lax.dynamic_index_in_dim(a, source, 0, False), gathered)

    return lax.fori_loop(
        1, lax.axis_size(axis), lambda source, state: combine(state, take(source)), take(0)
    )


def joint_stats(first, second):
    peak = jnp.maximum(first[0], second[0])
    return (peak, first[1] * jnp.exp(first[0] - peak) + second[1] * jnp.exp(second[0] - peak))


def local(text_emb, image_emb, log_mass_src, log_mass_tgt, pair_blocks, pair_counts):
    block = BLK
    src_blocks = text_emb.shape[0] // block
    tgt_blocks = image_emb.shape[0] // block
    width = text_emb.shape[1]
    active = pair_counts[0]

    def fetch(slot):
        src_local = pair_blocks[slot, 0]
        tgt_local = pair_blocks[slot, 1]
        text_rows = lax.dynamic_slice_in_dim(text_emb, src_local * block, block, 0)
        image_rows = lax.dynamic_slice_in_dim(image_emb, tgt_local * block, block, 0)
        return (src_local, tgt_local, text_rows, image_rows)

    def compute(text_rows, image_rows):
        return (
            lax.dot_general(
                text_rows, image_rows, (((1,), (1,)), ((), ())), preferred_element_type=jnp.float32
            )
            * inv_temp
        )

    def scores(text_rows, image_rows):
        return compute(text_rows, image_rows)

    def rows_pass(tgt_pot):

        def rows_step(slot, carry):
            peak, total = carry
            src_local, tgt_local, text_rows, image_rows = fetch(slot)
            shifted = (
                scores(text_rows, image_rows)
                + lax.dynamic_slice_in_dim(tgt_pot, tgt_local * block, block, 0)[None, :]
            )
            tile_peak = jnp.max(shifted, axis=1)
            tile_total = jnp.sum(jnp.exp(shifted - tile_peak[:, None]), axis=1)
            older = (
                lax.dynamic_index_in_dim(peak, src_local, 0, keepdims=False),
                lax.dynamic_index_in_dim(total, src_local, 0, keepdims=False),
            )
            new_peak, new_total = joint_stats(older, (tile_peak, tile_total))
            return (
                lax.dynamic_update_index_in_dim(peak, new_peak, src_local, 0),
                lax.dynamic_update_index_in_dim(total, new_total, src_local, 0),
            )

        start = (
            jnp.full((src_blocks, block), floor_value, jnp.float32),
            jnp.zeros((src_blocks, block), jnp.float32),
        )
        peak, total = lax.fori_loop(0, active, rows_step, start)
        peak, total = merged((peak, total), "tgt", joint_stats)
        return log_mass_src - (peak + jnp.log(total)).reshape(-1)

    def cols_pass(src_pot):

        def cols_step(slot, carry):
            peak, total = carry
            src_local, tgt_local, text_rows, image_rows = fetch(slot)
            shifted = (
                scores(text_rows, image_rows)
                + lax.dynamic_slice_in_dim(src_pot, src_local * block, block, 0)[:, None]
            )
            tile_peak = jnp.max(shifted, axis=0)
            tile_total = jnp.sum(jnp.exp(shifted - tile_peak[None, :]), axis=0)
            older = (
                lax.dynamic_index_in_dim(peak, tgt_local, 0, keepdims=False),
                lax.dynamic_index_in_dim(total, tgt_local, 0, keepdims=False),
            )
            new_peak, new_total = joint_stats(older, (tile_peak, tile_total))
            return (
                lax.dynamic_update_index_in_dim(peak, new_peak, tgt_local, 0),
                lax.dynamic_update_index_in_dim(total, new_total, tgt_local, 0),
            )

        start = (
            jnp.full((tgt_blocks, block), floor_value, jnp.float32),
            jnp.zeros((tgt_blocks, block), jnp.float32),
        )
        peak, total = lax.fori_loop(0, active, cols_step, start)
        peak, total = merged((peak, total), "src", joint_stats)
        return log_mass_tgt - (peak + jnp.log(total)).reshape(-1)

    tgt_pot = jnp.zeros((tgt_blocks * block,), jnp.float32)
    src_pot = jnp.zeros((src_blocks * block,), jnp.float32)
    for step_index in range(ITERS):
        src_pot = rows_pass(tgt_pot)
        tgt_pot = cols_pass(src_pot)

    def plan_tile(slot):
        src_local, tgt_local, text_rows, image_rows = fetch(slot)
        src_part = lax.dynamic_slice_in_dim(src_pot, src_local * block, block, 0)
        tgt_part = lax.dynamic_slice_in_dim(tgt_pot, tgt_local * block, block, 0)
        plan = jnp.exp(scores(text_rows, image_rows) + src_part[:, None] + tgt_part[None, :])
        return (src_local, tgt_local, text_rows, image_rows, plan)

    def add_into(mass, numer, index, plan_sum, contrib):
        old_mass = lax.dynamic_slice_in_dim(mass, index * block, block, 0)
        mass = lax.dynamic_update_slice_in_dim(mass, old_mass + plan_sum, index * block, 0)
        old_numer = lax.dynamic_slice_in_dim(numer, index * block, block, 0)
        numer = lax.dynamic_update_slice_in_dim(numer, old_numer + contrib, index * block, 0)
        return (mass, numer)

    def row_terms(plan, image_rows):
        weight = plan.astype(jnp.bfloat16)
        return (
            jnp.sum(plan, axis=1),
            jnp.dot(weight, image_rows, preferred_element_type=jnp.float32),
        )

    def col_terms(plan, text_rows):
        weight = plan.astype(jnp.bfloat16)
        contrib = lax.dot_general(
            weight, text_rows, (((0,), (0,)), ((), ())), preferred_element_type=jnp.float32
        )
        return (jnp.sum(plan, axis=0), contrib)

    def add_rows(slot, carry):
        src_local, tgt_local, text_rows, image_rows, plan = plan_tile(slot)
        plan_sum, contrib = row_terms(plan, image_rows)
        return add_into(carry[0], carry[1], src_local, plan_sum, contrib)

    def add_cols(slot, carry):
        src_local, tgt_local, text_rows, image_rows, plan = plan_tile(slot)
        plan_sum, contrib = col_terms(plan, text_rows)
        return add_into(carry[0], carry[1], tgt_local, plan_sum, contrib)

    src_start = (
        jnp.zeros((src_blocks * block,), jnp.float32),
        jnp.zeros((src_blocks * block, width), jnp.float32),
    )
    tgt_start = (
        jnp.zeros((tgt_blocks * block,), jnp.float32),
        jnp.zeros((tgt_blocks * block, width), jnp.float32),
    )
    tgt_mass, tgt_numer = lax.fori_loop(0, active, add_cols, tgt_start)
    mass = tgt_mass
    numer = tgt_numer
    numer, mass = (
        lax.psum_scatter(numer, "src", scatter_dimension=0, tiled=True),
        lax.psum_scatter(mass, "src", scatter_dimension=0, tiled=True),
    )
    tgt_map = numer / mass[:, None]
    src_mass, src_numer = lax.fori_loop(0, active, add_rows, src_start)
    mass = src_mass
    numer = src_numer
    numer, mass = (
        lax.psum_scatter(numer, "tgt", scatter_dimension=0, tiled=True),
        lax.psum_scatter(mass, "tgt", scatter_dimension=0, tiled=True),
    )
    src_map = numer / mass[:, None]
    return (src_map, tgt_map)


def solution(mesh):
    return jax.shard_map(
        local,
        mesh=mesh,
        in_specs=(
            P("src", None),
            P("tgt", None),
            P("src"),
            P("tgt"),
            P(("src", "tgt"), None),
            P(("src", "tgt")),
        ),
        out_specs=(P(("src", "tgt"), None), P(("tgt", "src"), None)),
        check_vma=False,
    )
```

profile of v0, /device:TPU:0, one launch (start us, length us, event | category | flops | bytes accessed | tf_op | source)
XLA Modules:
  0.0 1131.5 jit_solution(14129859163921226931)
XLA Ops:
  7.2 20.9 %while.198 = (s32[]{:T(128)}, f32[8,256]{1,0:T(8,128)S(1)}, f32[8,256]{1,0:T(8,128)S(1)}, s32[]{:T(128)}, s32[16,2]{0,1:T(2,128)}, /*index=5*/bf16[2048,512]{1,0...) while((s32[]{:T(128)}, f32[8,256]{1,0:T(8,128)S(1)}, ...), condition=%wide.region_3.4_spmd, body=%wide.region_0.3_spmd.sunk | while | flops 67372048 | bytes 1062221 | solution.py:80
  28.2 5.2 all-gather
  33.4 5.2 all-gather.1
  38.7 21.7 %while.200 = (s32[]{:T(128)}, f32[8,256]{1,0:T(8,128)S(1)}, f32[8,256]{1,0:T(8,128)S(1)}, s32[]{:T(128)}, s32[16,2]{0,1:T(2,128)}, /*index=5*/bf16[2048,512]{1,0...) while((s32[]{:T(128)}, f32[8,256]{1,0:T(8,128)S(1)}, ...), condition=%wide.region_9.10_spmd, body=%wide.region_6.9_spmd.sunk | while | flops 67437584 | bytes 1065305 | solution.py:109
  60.5 209.5 %all-gather.2 = f32[64,256]{1,0:T(8,128)S(1)} all-gather(f32[8,256]{1,0:T(8,128)S(1)} %get-tuple-element.1161), channel_id=4, replica_groups=mesh['src'=8,'tgt'=4] {'src'}, dimensions={0}, use_global_device_ids=true | all-gather | bytes 73728 | tf_op jit(solution)/shard_map/all_gather | solution.py:15
  270.0 30.5 %all-gather.3 = f32[64,256]{1,0:T(8,128)S(1)} all-gather(f32[8,256]{1,0:T(8,128)S(1)} %get-tuple-element.1162), channel_id=5, replica_groups=mesh['src'=8,'tgt'=4] {'src'}, dimensions={0}, use_global_device_ids=true | all-gather | bytes 73728 | tf_op jit(solution)/shard_map/all_gather | solution.py:15
  300.9 21.7 %while.202 = (s32[]{:T(128)}, f32[8,256]{1,0:T(8,128)S(1)}, f32[8,256]{1,0:T(8,128)S(1)}, s32[]{:T(128)}, s32[16,2]{0,1:T(2,128)}, /*index=5*/bf16[2048,512]{1,0...) while((s32[]{:T(128)}, f32[8,256]{1,0:T(8,128)S(1)}, ...), condition=%wide.region_15.16_spmd, body=%wide.region_12.15_spmd.sunk | while | flops 67437584 | bytes 1065305 | solution.py:80
  322.5 5.2 all-gather.4
  327.7 5.2 all-gather.5
  333.1 20.6 %while.204 = (s32[]{:T(128)}, f32[8,256]{1,0:T(8,128)S(1)}, f32[8,256]{1,0:T(8,128)S(1)}, s32[]{:T(128)}, s32[16,2]{0,1:T(2,128)}, /*index=5*/bf16[2048,512]{1,0...) while((s32[]{:T(128)}, f32[8,256]{1,0:T(8,128)S(1)}, ...), condition=%wide.region_21.22_spmd, body=%wide.region_18.21_spmd.sunk | while | flops 67437584 | bytes 1065305 | solution.py:109
  353.7 203.6 %all-gather.6 = f32[64,256]{1,0:T(8,128)S(1)} all-gather(f32[8,256]{1,0:T(8,128)S(1)} %get-tuple-element.1169), channel_id=8, replica_groups=mesh['src'=8,'tgt'=4] {'src'}, dimensions={0}, use_global_device_ids=true | all-gather | bytes 73728 | tf_op jit(solution)/shard_map/all_gather | solution.py:15
  557.3 30.5 %all-gather.7 = f32[64,256]{1,0:T(8,128)S(1)} all-gather(f32[8,256]{1,0:T(8,128)S(1)} %get-tuple-element.1170), channel_id=9, replica_groups=mesh['src'=8,'tgt'=4] {'src'}, dimensions={0}, use_global_device_ids=true | all-gather | bytes 73728 | tf_op jit(solution)/shard_map/all_gather | solution.py:15
  588.1 21.1 %while.206 = (s32[]{:T(128)}, f32[8,256]{1,0:T(8,128)S(1)}, f32[8,256]{1,0:T(8,128)S(1)}, s32[]{:T(128)}, s32[16,2]{0,1:T(2,128)}, /*index=5*/bf16[2048,512]{1,0...) while((s32[]{:T(128)}, f32[8,256]{1,0:T(8,128)S(1)}, ...), condition=%wide.region_27.28_spmd, body=%wide.region_24.27_spmd.sunk | while | flops 67437584 | bytes 1065305 | solution.py:80
  609.2 5.2 all-gather.8
  614.4 5.2 all-gather.9
  619.8 20.2 %while.208 = (s32[]{:T(128)}, f32[8,256]{1,0:T(8,128)S(1)}, f32[8,256]{1,0:T(8,128)S(1)}, s32[]{:T(128)}, s32[16,2]{0,1:T(2,128)}, /*index=5*/bf16[2048,512]{1,0...) while((s32[]{:T(128)}, f32[8,256]{1,0:T(8,128)S(1)}, ...), condition=%wide.region_33.34_spmd, body=%wide.region_30.33_spmd.sunk | while | flops 67437584 | bytes 1065305 | solution.py:109
  640.0 199.2 %all-gather.10 = f32[64,256]{1,0:T(8,128)S(1)} all-gather(f32[8,256]{1,0:T(8,128)S(1)} %get-tuple-element.1177), channel_id=12, replica_groups=mesh['src'=8,'tgt'=4] {'src'}, dimensions={0}, use_global_device_ids=true | all-gather | bytes 73728 | tf_op jit(solution)/shard_map/all_gather | solution.py:15
  839.1 30.5 %all-gather.11 = f32[64,256]{1,0:T(8,128)S(1)} all-gather(f32[8,256]{1,0:T(8,128)S(1)} %get-tuple-element.1178), channel_id=13, replica_groups=mesh['src'=8,'tgt'=4] {'src'}, dimensions={0}, use_global_device_ids=true | all-gather | bytes 73728 | tf_op jit(solution)/shard_map/all_gather | solution.py:15
  869.9 2.5 broadcast.54.clone.1
  872.5 20.2 %while.211 = (s32[]{:T(128)}, f32[2048]{0:T(1024)S(1)}, f32[2048,512]{1,0:T(8,128)}, s32[]{:T(128)}, s32[16,2]{0,1:T(2,128)S(1)}, /*index=5*/bf16[2048,512]{1,0:...) while((s32[]{:T(128)}, f32[2048]{0:T(1024)S(1)}, ...), condition=%wide.region_43.44_spmd, body=%wide.region_41.43_spmd.sunk | while | flops 134676496 | bytes 2107699 | solution.py:165
  895.2 19.6 %while.210 = (s32[]{:T(128)}, f32[2048]{0:T(1024)S(1)}, f32[2048,512]{1,0:T(8,128)}, s32[]{:T(128)}, s32[16,2]{0,1:T(2,128)S(1)}, /*index=5*/bf16[2048,512]{1,0:...) while((s32[]{:T(128)}, f32[2048]{0:T(1024)S(1)}, ...), condition=%wide.region_38.39_spmd, body=%wide.region_36.38_spmd.sunk | while | flops 134676496 | bytes 2107699 | solution.py:173
  917.2 180.1 %all-reduce.1 = f32[2048]{0:T(1024)S(1)} all-reduce(f32[2048]{0:T(1024)S(1)} %get-tuple-element.1184), channel_id=17, replica_groups=mesh['src'=8,'tgt'=4] {'src'}, use_global_device_ids=true, to_apply=%region_45.46.clone | all-reduce | flops 2048 | bytes 16384
  1098.1 6.5 all-reduce
  1106.6 15.7 %reduce-scatter.3.cloned.1.call-done = f32[512,512]{1,0:T(8,128)} async-done(((f32[2048,512]{1,0:T(8,128)}), f32[512,512]{1,0:T(8,128)}) %reduce-scatter.3.cloned.1.call-update) | async-done | bytes 1048592 | tf_op jit(solution)/shard_map/reduce_scatter | solution.py:177
  (261 shorter events, 90.2 us)
Async XLA Ops:
  7.2 1097.5 %reduce-scatter.5.cloned.1.call-start = ((), (), s32[]{:S(2)}) async-start(), calls=%async_computation.3 | async-start | bytes 4718592 | tf_op jit(solution)/shard_map/reduce_scatter | solution.py:169
  7.2 31.5 %copy-start.1 = (f32[2048]{0:T(1024)S(1)}, f32[2048]{0:T(1024)}, u32[]{:S(2)}) copy-start(f32[2048]{0:T(1024)} %param.36) | copy-start | bytes 24580
  38.7 262.1 %copy-start.2 = (f32[2048]{0:T(1024)S(1)}, f32[2048]{0:T(1024)}, u32[]{:S(2)}) copy-start(f32[2048]{0:T(1024)} %param.37) | copy-start | bytes 24580
  869.9 2.5 copy-start
  892.7 229.6 %reduce-scatter.3.cloned.1.call-start = ((), (), s32[]{:S(2)}) async-start(), calls=%async_computation.2 | async-start | bytes 5242880 | tf_op jit(solution)/shard_map/reduce_scatter | solution.py:177
  914.8 0.7 copy-start.4
  914.8 1.2 copy-start.3
Sparse Core Ops, SparseCore 0:
  892.8 168.3 reduce-scatter.4
  1063.9 58.4 reduce-scatter.2
where the time goes:
time: 1150 us; the launch traced here: 1130 us
  blocking collectives  921 us (80%)
  loops' own time  87 us (8%)
  matrix products  44.5 us (4%)
  local copies, waits for them, and re-layouts  39.5 us (3%)
  between operations  15.8 us (1%)
  waiting for transfers between devices  15.7 us (1%)
    all_gather x12, blocking collectives, merged(): gathered = jax.tree.map(lambda a: lax.all_gather(a, axis), part)  735 us
    unnamed x2, blocking collectives  187 us
    another operation x3, loops' own time, rows_pass(): peak, total = lax.fori_loop(0, active, rows_step, start)  37.2 us
    another operation x3, loops' own time, cols_pass(): peak, total = lax.fori_loop(0, active, cols_step, start)  36.1 us
    dot_general x24, matrix products, compute(): lax.dot_general(text_rows, image_rows, (((1,), (1,)), ((), ())), preferre...  31.4 us
    dynamic_slice x21, local copies, waits for them, and re-layouts, fetch(): src_local = pair_blocks[slot, 0]  27.1 us
  transfers between devices with their start and end apart: 2, of which 1 were waited for; matrix products, arithmetic and copies ran while one was open for 2% of the time, Pallas kernels for 0%

commit v1 on v0

v1 whole, which is shorter than its diff:
```python
import functools

import jax
import jax.numpy as jnp
from jax import lax
from jax.experimental import pallas as pl
from jax.experimental.pallas import tpu as pltpu
from jax.sharding import PartitionSpec as P

BLK = 256
ITERS = 3
LANES = 128

inv_temp = 0.15
floor_value = -1e30
MESH = pl.DeviceIdType.MESH


def each(low, high, body):
    if high - low <= 8:
        for i in range(low, high):
            body(i)
    else:

        def step(i, carry):
            body(i)
            return carry

        lax.fori_loop(low, high, step, 0)


def looped(low, high, body, unroll=1):

    def step(i, carry):
        body(i)
        return carry

    lax.fori_loop(low, high, step, 0, unroll=unroll)


def partner(me, n, step):
    if n & (n - 1):
        return lax.rem(me + 1 + step, n)
    mask = n - 1 - step
    out = me * 0
    bit = 1
    while bit < n:
        out = out + ((me // bit + mask // bit) % 2) * bit
        bit *= 2
    return out


def kernel(
    n_src, n_tgt, inner,
    pairs, count, slots, text, image, mass_src, mass_tgt,
    src_out, tgt_out,
    score, score_t, weight, weight_t, bias_src, bias_tgt,
    src_wide, tgt_wide, src_row, tgt_row, top, tot,
    src_parts, tgt_parts,
    pair_send, pair_got, outer_sum, outer_got, part_send, part_got,
    src_ss, src_rs, tgt_ss, tgt_rs,
    pair_ss, pair_rs, outer_ss, outer_rs, part_ss, part_rs,
):
    cap = score.shape[0]
    sb, block, width = text.shape
    tb = image.shape[0]
    s = lax.axis_index("src")
    t = lax.axis_index("tgt")
    n_outer = n_src // inner
    outer, side = s // inner, s % inner
    mate = outer * inner + (inner - 1 - side)

    def greet(device):
        pl.semaphore_signal(barrier, inc=1, device_id=device, device_id_type=MESH)

    barrier = pltpu.get_barrier_semaphore()
    each(1, n_tgt, lambda d: greet((s, (t + d) % n_tgt)))
    each(1, n_src, lambda d: greet(((s + d) % n_src, t)))

    def make_bias(k):
        used = k < count[0]
        rows = lax.broadcasted_iota(jnp.int32, (sb, block), 0)
        a = jnp.where(used, pairs[k, 0], -1)
        bias_src[k] = jnp.where(rows == a, 0.0, floor_value)
        cols = lax.broadcasted_iota(jnp.int32, (tb, block), 0)
        b = jnp.where(used, pairs[k, 1], -1)
        bias_tgt[k] = jnp.where(cols == b, 0.0, floor_value)

    def make_scores(k):
        make_bias(k)
        rows, cols = text[pairs[k, 0]], image[pairs[k, 1]]
        nt = (((1,), (1,)), ((), ()))
        score[k] = lax.dot_general(rows, cols, nt, preferred_element_type=jnp.float32) * inv_temp
        score_t[k] = lax.dot_general(cols, rows, nt, preferred_element_type=jnp.float32) * inv_temp

    looped(0, cap, make_scores)
    tgt_wide[...] = jnp.zeros_like(tgt_wide)
    pl.semaphore_wait(barrier, n_tgt - 1 + n_src - 1)

    def push(parts, step, me, n, device, ss, rs, d):
        return pltpu.make_async_remote_copy(
            src_ref=parts.at[step, me],
            dst_ref=parts.at[step, me],
            send_sem=ss.at[step, d],
            recv_sem=rs.at[step, me],
            device_id=device,
            device_id_type=MESH,
        )

    def arrival(parts, step, d, me, n, device, ss, rs):
        other = (me + d) % n
        return pltpu.make_async_remote_copy(
            src_ref=parts.at[step, other],
            dst_ref=parts.at[step, other],
            send_sem=ss.at[step, d],
            recv_sem=rs.at[step, other],
            device_id=device,
            device_id_type=MESH,
        )

    def src_group(d):
        return (s, (t + d) % n_tgt)

    def tgt_group(d):
        return ((s + d) % n_src, t)

    sides = {
        "src": (src_parts, t, n_tgt, src_group, src_ss, src_rs),
        "tgt": (tgt_parts, s, n_src, tgt_group, tgt_ss, tgt_rs),
    }

    def send_parts(which, step):
        parts, me, n, group, ss, rs = sides[which]
        each(1, n, lambda d: push(parts, step, me, n, group(d), ss, rs, d).start())

    def wait_parts(which, step):
        parts, me, n, group, ss, rs = sides[which]
        each(1, n, lambda d: arrival(parts, step, d, me, n, group(d), ss, rs).wait_recv())
        each(1, n, lambda d: push(parts, step, me, n, group(d), ss, rs, d).wait_send())

    def lse_pass(tiles, wide, column):

        def one(k):
            shift = wide[pairs[k, column]]
            for h in range(block // LANES):
                lanes = pl.ds(h * LANES, LANES)
                shifted = (tiles[k, :, lanes] + shift).reshape(block // 8, 8, LANES)
                peak = jnp.max(shifted, axis=0)
                top[k, :, lanes] = peak
                tot[k, :, lanes] = jnp.sum(jnp.exp(shifted - peak[None]), axis=0)

        looped(0, cap, one, unroll=2)

    def local_part(bias):
        peaks = top[...]
        peak = jnp.max(peaks, axis=1, keepdims=True)
        total = jnp.sum(tot[...] * jnp.exp(peaks - peak), axis=1, keepdims=True)
        masked = (peak + jnp.log(total)) + bias[...]
        highest = jnp.max(masked, axis=0)
        return highest + jnp.log(jnp.sum(jnp.exp(masked - highest[None]), axis=0))

    def merged(parts, step):
        every = parts[step]
        highest = jnp.max(every, axis=0)
        return highest + jnp.log(jnp.sum(jnp.exp(every - highest[None]), axis=0))

    def widen(value, wide):
        columns = value.T
        for c in range(value.shape[0]):
            wide[c] = jnp.broadcast_to(columns[:, c : c + 1], (block, LANES))

    def spread(value, row):
        for c in range(value.shape[0]):
            row[c] = value[c : c + 1, :]

    def iterate(step):
        lse_pass(score_t, tgt_wide, 1)
        src_parts[step, t] = local_part(bias_src)
        send_parts("src", step)
        wait_parts("src", step)
        pot = mass_src[...] - merged(src_parts, step)
        widen(pot, src_wide)
        spread(pot, src_row)
        lse_pass(score, src_wide, 0)
        tgt_parts[step, s] = local_part(bias_tgt)
        send_parts("tgt", step)
        wait_parts("tgt", step)
        pot = mass_tgt[...] - merged(tgt_parts, step)
        widen(pot, tgt_wide)
        spread(pot, tgt_row)

    looped(0, ITERS, iterate)

    def plan(k):
        a, b = pairs[k, 0], pairs[k, 1]
        for h in range(block // LANES):
            lanes = pl.ds(h * LANES, LANES)
            tile = score[k, :, lanes] + src_wide[a] + tgt_row[b, :, lanes]
            tile = jnp.exp(tile)
            weight[k, :, lanes] = tile.astype(jnp.bfloat16)
            top[k, :, lanes] = jnp.sum(tile.reshape(block // 8, 8, LANES), axis=0)
            tile = score_t[k, :, lanes] + src_row[a, :, lanes] + tgt_wide[b]
            tile = jnp.exp(tile)
            weight_t[k, :, lanes] = tile.astype(jnp.bfloat16)
            tot[k, :, lanes] = jnp.sum(tile.reshape(block // 8, 8, LANES), axis=0)

    looped(0, cap, plan)
    weight[cap] = jnp.zeros(weight.shape[1:], weight.dtype)
    weight_t[cap] = jnp.zeros(weight_t.shape[1:], weight_t.dtype)

    def mass_part(sums, bias):
        rows = jnp.sum(sums[...], axis=1, keepdims=True)
        return jnp.sum(jnp.where(bias[...] == 0.0, rows, 0.0), axis=0)

    src_parts[ITERS, t] = mass_part(tot, bias_src)
    tgt_parts[ITERS, s] = mass_part(top, bias_tgt)
    send_parts("tgt", ITERS)
    send_parts("src", ITERS)

    def unit_rows(n, clusters):
        own = clusters * block // n
        return own, min(own, block)

    tgt_own, tgt_unit = unit_rows(n_src, tb)
    src_own, src_unit = unit_rows(n_tgt, sb)

    def numer(start, unit, tiles, index, count_other, table):
        cluster, off = start // block, start % block
        picks = []
        for c in range(count_other):
            slot = slots[index(cluster, c)]
            if unit == block:
                picks.append(tiles[slot])
            else:
                picks.append(tiles[slot, pl.ds(pl.multiple_of(off, unit), unit), :])
        left = jnp.concatenate(picks, axis=1)
        right = table[...].reshape(count_other * block, width)
        return jnp.dot(left, right, preferred_element_type=jnp.float32)

    def tgt_numer(owner, out, where):
        for u in range(tgt_own // tgt_unit):
            start = owner * tgt_own + u * tgt_unit
            out[where, pl.ds(u * tgt_unit, tgt_unit), :] = numer(
                start, tgt_unit, weight_t, lambda j, a: a * tb + j, sb, text
            )

    def src_numer(owner, out, where):

        def unit(u):
            start = owner * src_own + u * src_unit
            rows = pl.ds(pl.multiple_of(u * src_unit, src_unit), src_unit)
            out[where, rows, :] = numer(start, src_unit, weight, lambda i, b: i * tb + b, tb, image)

        looped(0, src_own // src_unit, unit)

    def pair_copy(z):
        return pltpu.make_async_remote_copy(
            src_ref=pair_send.at[z],
            dst_ref=pair_got.at[z],
            send_sem=pair_ss.at[z],
            recv_sem=pair_rs.at[z],
            device_id=(mate, t),
            device_id_type=MESH,
        )

    def outer_copy(z, slot):
        return pltpu.make_async_remote_copy(
            src_ref=outer_sum.at[z],
            dst_ref=outer_got.at[slot],
            send_sem=outer_ss.at[z],
            recv_sem=outer_rs.at[slot],
            device_id=(z * inner + side, t),
            device_id_type=MESH,
        )

    def part_copy(other, slot):
        return pltpu.make_async_remote_copy(
            src_ref=part_send.at[other],
            dst_ref=part_got.at[slot],
            send_sem=part_ss.at[other],
            recv_sem=part_rs.at[slot],
            device_id=(s, other),
            device_id_type=MESH,
        )

    def to_mate(step):
        z = partner(outer, n_outer, step)
        tgt_numer(z * inner + (inner - 1 - side), pair_send, z)
        pair_copy(z).start()

    def to_part(step):
        other = partner(t, n_tgt, step)
        src_numer(other, part_send, other)
        part_copy(other, t).start()

    def own_outer(step):
        z = partner(outer, n_outer, step)
        tgt_numer(z * inner + side, outer_sum, z)

    if inner == 2:
        looped(0, n_outer, to_mate)
    looped(0, n_tgt - 1, to_part)
    looped(0, n_outer, own_outer)

    def forward(step):
        z = partner(outer, n_outer, step)
        if inner == 2:
            pair_copy(z).wait_recv()
            outer_sum[z] = outer_sum[z] + pair_got[z]
        outer_copy(z, outer).start()

    looped(0, n_outer - 1, forward)
    src_numer(t, part_send, t)

    wait_parts("src", ITERS)
    wait_parts("tgt", ITERS)
    widen(jnp.sum(src_parts[ITERS], axis=0), src_wide)
    widen(jnp.sum(tgt_parts[ITERS], axis=0), tgt_wide)

    def take_part(step):
        other = partner(t, n_tgt, step)
        part_copy(other, other).wait_recv()
        part_send[t] = part_send[t] + part_got[other]

    looped(0, n_tgt - 1, take_part)
    for u in range(src_own // src_unit):
        start = t * src_own + u * src_unit
        rows = pl.ds(u * src_unit, src_unit)
        off = pl.multiple_of(start % block, src_unit)
        mass = src_wide[start // block, pl.ds(off, src_unit), :]
        for c in range(width // LANES):
            lanes = pl.ds(c * LANES, LANES)
            src_out[rows, lanes] = part_send[t, rows, lanes] / mass

    if inner == 2:
        pair_copy(outer).wait_recv()
        outer_sum[outer] = outer_sum[outer] + pair_got[outer]

    def take_outer(step):
        z = partner(outer, n_outer, step)
        outer_copy(z, z).wait_recv()
        outer_sum[outer] = outer_sum[outer] + outer_got[z]

    looped(0, n_outer - 1, take_outer)
    for u in range(tgt_own // tgt_unit):
        start = s * tgt_own + u * tgt_unit
        rows = pl.ds(u * tgt_unit, tgt_unit)
        off = pl.multiple_of(start % block, tgt_unit)
        mass = tgt_wide[start // block, pl.ds(off, tgt_unit), :]
        for c in range(width // LANES):
            lanes = pl.ds(c * LANES, LANES)
            tgt_out[rows, lanes] = outer_sum[outer, rows, lanes] / mass

    def sent_pair(step):
        pair_copy(partner(outer, n_outer, step)).wait_send()

    def sent_outer(step):
        outer_copy(partner(outer, n_outer, step), outer).wait_send()

    def sent_part(step):
        part_copy(partner(t, n_tgt, step), t).wait_send()

    if inner == 2:
        looped(0, n_outer, sent_pair)
    looped(0, n_outer - 1, sent_outer)
    looped(0, n_tgt - 1, sent_part)


def local(n_src, n_tgt, text_emb, image_emb, log_mass_src, log_mass_tgt, pair_blocks, pair_counts):
    sb = text_emb.shape[0] // BLK
    tb = image_emb.shape[0] // BLK
    width = text_emb.shape[1]
    cap = pair_blocks.shape[0]
    inner = 2 if n_src % 2 == 0 else 1
    n_outer = n_src // inner
    tgt_own = tb * BLK // n_src
    src_own = sb * BLK // n_tgt

    slot_ids = jnp.arange(cap, dtype=jnp.int32)
    combo = jnp.where(slot_ids < pair_counts[0], pair_blocks[:, 0] * tb + pair_blocks[:, 1], -1)
    combos = jnp.arange(sb * tb, dtype=jnp.int32)
    slots = jnp.min(jnp.where(combo[None, :] == combos[:, None], slot_ids[None, :], cap), axis=1)

    f32, bf16 = jnp.float32, jnp.bfloat16
    dma = pltpu.SemaphoreType.DMA
    smem = pl.BlockSpec(memory_space=pltpu.SMEM)
    vmem = pl.BlockSpec(memory_space=pltpu.VMEM)
    return pl.pallas_call(
        functools.partial(kernel, n_src, n_tgt, inner),
        out_shape=(
            jax.ShapeDtypeStruct((src_own, width), f32),
            jax.ShapeDtypeStruct((tgt_own, width), f32),
        ),
        in_specs=[smem] * 3 + [vmem] * 4,
        out_specs=(vmem, vmem),
        scratch_shapes=[
            pltpu.VMEM((cap, BLK, BLK), f32),
            pltpu.VMEM((cap, BLK, BLK), f32),
            pltpu.VMEM((cap + 1, BLK, BLK), bf16),
            pltpu.VMEM((cap + 1, BLK, BLK), bf16),
            pltpu.VMEM((cap, sb, BLK), f32),
            pltpu.VMEM((cap, tb, BLK), f32),
            pltpu.VMEM((sb, BLK, LANES), f32),
            pltpu.VMEM((tb, BLK, LANES), f32),
            pltpu.VMEM((sb, 1, BLK), f32),
            pltpu.VMEM((tb, 1, BLK), f32),
            pltpu.VMEM((cap, 8, BLK), f32),
            pltpu.VMEM((cap, 8, BLK), f32),
            pltpu.VMEM((ITERS + 1, n_tgt, sb, BLK), f32),
            pltpu.VMEM((ITERS + 1, n_src, tb, BLK), f32),
            pltpu.VMEM((n_outer, tgt_own, width), f32),
            pltpu.VMEM((n_outer, tgt_own, width), f32),
            pltpu.VMEM((n_outer, tgt_own, width), f32),
            pltpu.VMEM((n_outer, tgt_own, width), f32),
            pltpu.VMEM((n_tgt, src_own, width), f32),
            pltpu.VMEM((n_tgt, src_own, width), f32),
            dma((ITERS + 1, n_tgt)),
            dma((ITERS + 1, n_tgt)),
            dma((ITERS + 1, n_src)),
            dma((ITERS + 1, n_src)),
            dma((n_outer,)),
            dma((n_outer,)),
            dma((n_outer,)),
            dma((n_outer,)),
            dma((n_tgt,)),
            dma((n_tgt,)),
        ],
        compiler_params=pltpu.CompilerParams(
            collective_id=0, has_side_effects=True, vmem_limit_bytes=50 * 1024 * 1024
        ),
    )(
        pair_blocks,
        pair_counts,
        slots,
        text_emb.reshape(sb, BLK, width),
        image_emb.reshape(tb, BLK, width),
        log_mass_src.reshape(sb, BLK),
        log_mass_tgt.reshape(tb, BLK),
    )


def solution(mesh):
    n_src, n_tgt = mesh.shape["src"], mesh.shape["tgt"]
    return jax.shard_map(
        functools.partial(local, n_src, n_tgt),
        mesh=mesh,
        in_specs=(
            P("src", None),
            P("tgt", None),
            P("src"),
            P("tgt"),
            P(("src", "tgt"), None),
            P(("src", "tgt")),
        ),
        out_specs=(P(("src", "tgt"), None), P(("tgt", "src"), None)),
        check_vma=False,
    )
```

time: 1150 us -> 113 us (0.10); the launches traced: 1130 us -> 113 us
  blocking collectives: 921 us -> 0 us
  Pallas kernels: 0 us -> 105 us
  loops' own time: 87 us -> 0 us
  matrix products: 44.5 us -> 0 us
  local copies, waits for them, and re-layouts: 39.5 us -> 5.51 us
  waiting for transfers between devices: 15.7 us -> 0 us
  between operations: 15.8 us -> 1.29 us
    all_gather x12 -> x0, blocking collectives: 735 us -> none  [merged(): gathered = jax.tree.map(lambda a: lax.all_gather(a, axis), part)]
    unnamed x2 -> x0, blocking collectives: 187 us -> none
    pallas_call x0 -> x1, Pallas kernels: none -> 105 us  [local(): pl.pallas_call(functools.partial(kernel, n_src, n_tgt, inner), out_shape=...]
    another operation x14 -> x0, loops' own time: 87 us -> none  [the longest x3 37.2 us: rows_pass(): peak, total = lax.fori_loop(0, active, rows_step, start)]
    dot_general x30 -> x0, matrix products: 44.5 us -> none  [the longest x24 31.4 us: compute(): lax.dot_general(text_rows, image_rows, (((1,), (1,)), ((), ())), preferre...]
    dynamic_slice x63 -> x0, local copies, waits for them, and re-layouts: 31 us -> none  [the longest x21 27.1 us: fetch(): src_local = pair_blocks[slot, 0]]
    reduce_scatter x2 -> x0, waiting for transfers between devices: 15.7 us -> none  [the longest x1 15.7 us: local(): lax.psum_scatter(numer, 'tgt', scatter_dimension=0, tiled=True)]
  transfers between devices with their start and end apart: 2 -> 0, of which waited for: 1 -> 0; matrix products, arithmetic and copies ran while one was open for 2% -> 0% of each run, Pallas kernels for 0% -> 0%
where the time goes in v1:
time: 113 us
  Pallas kernels  105 us (93%)
  local copies, waits for them, and re-layouts  5.51 us (5%)
  between operations  1.29 us (1%)
    pallas_call x1, Pallas kernels, local(): pl.pallas_call(functools.partial(kernel, n_src, n_tgt, inner), out_shape=...  105 us
    unnamed x5, local copies, waits for them, and re-layouts  4.11 us

profile of v1, /device:TPU:0, one launch (start us, length us, event | category | flops | bytes accessed | tf_op | source)
XLA Modules:
  0.0 112.6 jit_solution(2854497847683333492)
XLA Ops:
  1.3 0.8 compare_select_fusion
  2.0 0.1 select_reduce_fusion.slots
  2.1 0.7 reshape.36.mass_src
  2.8 0.7 reshape.37.mass_tgt
  3.5 0.8 copy.9.pairs
  4.3 0.0 copy-start
  4.3 1.6 %copy-done = bf16[2048,512]{1,0:T(8,128)(2,1)S(1)} copy-done((bf16[2048,512]{1,0:T(8,128)(2,1)S(1)}, bf16[2048,512]{1,0:T(8,128)(2,1)}, u32[]{:S(2)}) %copy-start) | copy-done | bytes 2097176
  5.9 105.0 %shard_map.77 = (f32[512,512]{1,0:T(8,128)S(1)}, f32[256,512]{1,0:T(8,128)S(1)}) custom-call(s32[16,2]{1,0:T(8,128)S(1)} %copy.9.pairs, s32[1]{0:T(128)} %copy.12.count, s32[64]{0:T(128)S(1)} %select_reduce_fusion.slots, bf16[8,256,512]{2,1,0:T(8,128)(2,1)S(1)} %bitcast.6, bf16[8,256,512]{2,1,0:T(8,128)(2,1)} %bitcast.7, f32[8,256]{1,0:T(8,128)S(1)} %reshape.36.mass_src, ...), custom_call_target="tpu_custom_call" | custom-call | tf_op jit(solution)/shard_map/pallas_call | solution.py:388
  110.8 1.0 copy.13
  111.8 0.8 copy.14
Async XLA Ops:
  4.3 1.6 %copy-start = (bf16[2048,512]{1,0:T(8,128)(2,1)S(1)}, bf16[2048,512]{1,0:T(8,128)(2,1)}, u32[]{:S(2)}) copy-start(bf16[2048,512]{1,0:T(8,128)(2,1)} %param.6) | copy-start | bytes 6291460

commit v2 on v1

--- a/solution.py
+++ b/solution.py
@@ -52,14 +52,15 @@
 
 def kernel(
     n_src, n_tgt, inner,
-    pairs, count, slots, text, image, mass_src, mass_tgt,
+    codes, slots, text_hbm, image_hbm, lines_src, lines_tgt,
     src_out, tgt_out,
+    text, image, mass_src, mass_tgt,
     score, score_t, weight, weight_t, bias_src, bias_tgt,
     src_wide, tgt_wide, src_row, tgt_row, top, tot,
     src_parts, tgt_parts,
     pair_send, pair_got, outer_sum, outer_got, part_send, part_got,
     src_ss, src_rs, tgt_ss, tgt_rs,
-    pair_ss, pair_rs, outer_ss, outer_rs, part_ss, part_rs,
+    pair_ss, pair_rs, outer_ss, outer_rs, part_ss, part_rs, load_sem,
 ):
     cap = score.shape[0]
     sb, block, width = text.shape
@@ -73,27 +74,46 @@
     def greet(device):
         pl.semaphore_signal(barrier, inc=1, device_id=device, device_id_type=MESH)
 
+    loads = [
+        pltpu.make_async_copy(text_hbm, text, load_sem.at[0]),
+        pltpu.make_async_copy(image_hbm, image, load_sem.at[1]),
+    ]
+    for load in loads:
+        load.start()
     barrier = pltpu.get_barrier_semaphore()
     each(1, n_tgt, lambda d: greet((s, (t + d) % n_tgt)))
     each(1, n_src, lambda d: greet(((s + d) % n_src, t)))
 
+    def src_of(k):
+        return (codes[k] % (sb * tb)) // tb
+
+    def tgt_of(k):
+        return codes[k] % tb
+
     def make_bias(k):
-        used = k < count[0]
+        used = codes[k] < sb * tb
         rows = lax.broadcasted_iota(jnp.int32, (sb, block), 0)
-        a = jnp.where(used, pairs[k, 0], -1)
+        a = jnp.where(used, src_of(k), -1)
         bias_src[k] = jnp.where(rows == a, 0.0, floor_value)
         cols = lax.broadcasted_iota(jnp.int32, (tb, block), 0)
-        b = jnp.where(used, pairs[k, 1], -1)
+        b = jnp.where(used, tgt_of(k), -1)
         bias_tgt[k] = jnp.where(cols == b, 0.0, floor_value)
 
     def make_scores(k):
-        make_bias(k)
-        rows, cols = text[pairs[k, 0]], image[pairs[k, 1]]
+        rows, cols = text[src_of(k)], image[tgt_of(k)]
         nt = (((1,), (1,)), ((), ()))
         score[k] = lax.dot_general(rows, cols, nt, preferred_element_type=jnp.float32) * inv_temp
         score_t[k] = lax.dot_general(cols, rows, nt, preferred_element_type=jnp.float32) * inv_temp
 
-    looped(0, cap, make_scores)
+    looped(0, cap, make_bias)
+    for lines, mass in ((lines_src, mass_src), (lines_tgt, mass_tgt)):
+        for c in range(mass.shape[0]):
+            for h in range(block // LANES):
+                line = c * (block // LANES) + h
+                mass[c : c + 1, h * LANES : (h + 1) * LANES] = lines[line : line + 1, :]
+    for load in loads:
+        load.wait()
+    looped(0, cap, make_scores, unroll=2)
     tgt_wide[...] = jnp.zeros_like(tgt_wide)
     pl.semaphore_wait(barrier, n_tgt - 1 + n_src - 1)
 
@@ -138,10 +158,10 @@
         each(1, n, lambda d: arrival(parts, step, d, me, n, group(d), ss, rs).wait_recv())
         each(1, n, lambda d: push(parts, step, me, n, group(d), ss, rs, d).wait_send())
 
-    def lse_pass(tiles, wide, column):
+    def lse_pass(tiles, wide, cluster_of):
 
         def one(k):
-            shift = wide[pairs[k, column]]
+            shift = wide[cluster_of(k)]
             for h in range(block // LANES):
                 lanes = pl.ds(h * LANES, LANES)
                 shifted = (tiles[k, :, lanes] + shift).reshape(block // 8, 8, LANES)
@@ -149,7 +169,7 @@
                 top[k, :, lanes] = peak
                 tot[k, :, lanes] = jnp.sum(jnp.exp(shifted - peak[None]), axis=0)
 
-        looped(0, cap, one, unroll=2)
+        looped(0, cap, one, unroll=4)
 
     def local_part(bias):
         peaks = top[...]
@@ -174,14 +194,14 @@
             row[c] = value[c : c + 1, :]
 
     def iterate(step):
-        lse_pass(score_t, tgt_wide, 1)
+        lse_pass(score_t, tgt_wide, tgt_of)
         src_parts[step, t] = local_part(bias_src)
         send_parts("src", step)
         wait_parts("src", step)
         pot = mass_src[...] - merged(src_parts, step)
         widen(pot, src_wide)
         spread(pot, src_row)
-        lse_pass(score, src_wide, 0)
+        lse_pass(score, src_wide, src_of)
         tgt_parts[step, s] = local_part(bias_tgt)
         send_parts("tgt", step)
         wait_parts("tgt", step)
@@ -192,7 +212,7 @@
     looped(0, ITERS, iterate)
 
     def plan(k):
-        a, b = pairs[k, 0], pairs[k, 1]
+        a, b = src_of(k), tgt_of(k)
         for h in range(block // LANES):
             lanes = pl.ds(h * LANES, LANES)
             tile = score[k, :, lanes] + src_wide[a] + tgt_row[b, :, lanes]
@@ -204,7 +224,7 @@
             weight_t[k, :, lanes] = tile.astype(jnp.bfloat16)
             tot[k, :, lanes] = jnp.sum(tile.reshape(block // 8, 8, LANES), axis=0)
 
-    looped(0, cap, plan)
+    looped(0, cap, plan, unroll=2)
     weight[cap] = jnp.zeros(weight.shape[1:], weight.dtype)
     weight_t[cap] = jnp.zeros(weight_t.shape[1:], weight_t.dtype)
 
@@ -253,22 +273,34 @@
 
         looped(0, src_own // src_unit, unit)
 
-    def pair_copy(z):
+    halves = 2
+    ahead = 3
+    piece = tgt_own // halves
+    last = (n_outer - 1) * halves
+
+    def place(q):
+        rows = pl.ds(pl.multiple_of((q % halves) * piece, piece), piece)
+        return partner(outer, n_outer, q // halves), rows
+
+    def pair_copy(q):
+        z, rows = place(q)
         return pltpu.make_async_remote_copy(
-            src_ref=pair_send.at[z],
-            dst_ref=pair_got.at[z],
-            send_sem=pair_ss.at[z],
-            recv_sem=pair_rs.at[z],
+            src_ref=pair_send.at[z, rows],
+            dst_ref=pair_got.at[z, rows],
+            send_sem=pair_ss.at[z, q % halves],
+            recv_sem=pair_rs.at[z, q % halves],
             device_id=(mate, t),
             device_id_type=MESH,
         )
 
-    def outer_copy(z, slot):
+    def outer_copy(q, incoming=False):
+        z, rows = place(q)
+        slot = z if incoming else outer
         return pltpu.make_async_remote_copy(
-            src_ref=outer_sum.at[z],
-            dst_ref=outer_got.at[slot],
-            send_sem=outer_ss.at[z],
-            recv_sem=outer_rs.at[slot],
+            src_ref=outer_sum.at[z, rows],
+            dst_ref=outer_got.at[slot, rows],
+            send_sem=outer_ss.at[z, q % halves],
+            recv_sem=outer_rs.at[slot, q % halves],
             device_id=(z * inner + side, t),
             device_id_type=MESH,
         )
@@ -286,7 +318,9 @@
     def to_mate(step):
         z = partner(outer, n_outer, step)
         tgt_numer(z * inner + (inner - 1 - side), pair_send, z)
-        pair_copy(z).start()
+        for h in range(halves):
+            q = step * halves + h
+            pl.when(q < ahead)(lambda: pair_copy(q).start())
 
     def to_part(step):
         other = partner(t, n_tgt, step)
@@ -302,15 +336,20 @@
     looped(0, n_tgt - 1, to_part)
     looped(0, n_outer, own_outer)
 
-    def forward(step):
-        z = partner(outer, n_outer, step)
+    def collect(q):
         if inner == 2:
-            pair_copy(z).wait_recv()
-            outer_sum[z] = outer_sum[z] + pair_got[z]
-        outer_copy(z, outer).start()
-
-    looped(0, n_outer - 1, forward)
+            z, rows = place(q)
+            pair_copy(q).wait_recv()
+            pl.when(q + ahead < n_outer * halves)(lambda: pair_copy(q + ahead).start())
+            outer_sum[z, rows] = outer_sum[z, rows] + pair_got[z, rows]
+
+    def forward(q):
+        collect(q)
+        outer_copy(q).start()
+
+    looped(0, last, forward)
     src_numer(t, part_send, t)
+    looped(last, n_outer * halves, collect)
 
     wait_parts("src", ITERS)
     wait_parts("tgt", ITERS)
@@ -332,16 +371,12 @@
             lanes = pl.ds(c * LANES, LANES)
             src_out[rows, lanes] = part_send[t, rows, lanes] / mass
 
-    if inner == 2:
-        pair_copy(outer).wait_recv()
-        outer_sum[outer] = outer_sum[outer] + pair_got[outer]
-
-    def take_outer(step):
-        z = partner(outer, n_outer, step)
-        outer_copy(z, z).wait_recv()
-        outer_sum[outer] = outer_sum[outer] + outer_got[z]
-
-    looped(0, n_outer - 1, take_outer)
+    def take_outer(q):
+        z, rows = place(q)
+        outer_copy(q, incoming=True).wait_recv()
+        outer_sum[outer, rows] = outer_sum[outer, rows] + outer_got[z, rows]
+
+    looped(0, last, take_outer)
     for u in range(tgt_own // tgt_unit):
         start = s * tgt_own + u * tgt_unit
         rows = pl.ds(u * tgt_unit, tgt_unit)
@@ -351,18 +386,18 @@
             lanes = pl.ds(c * LANES, LANES)
             tgt_out[rows, lanes] = outer_sum[outer, rows, lanes] / mass
 
-    def sent_pair(step):
-        pair_copy(partner(outer, n_outer, step)).wait_send()
-
-    def sent_outer(step):
-        outer_copy(partner(outer, n_outer, step), outer).wait_send()
+    def sent_pair(q):
+        pair_copy(q).wait_send()
+
+    def sent_outer(q):
+        outer_copy(q).wait_send()
 
     def sent_part(step):
         part_copy(partner(t, n_tgt, step), t).wait_send()
 
     if inner == 2:
-        looped(0, n_outer, sent_pair)
-    looped(0, n_outer - 1, sent_outer)
+        looped(0, n_outer * halves, sent_pair)
+    looped(0, last, sent_outer)
     looped(0, n_tgt - 1, sent_part)
 
 
@@ -377,9 +412,10 @@
     src_own = sb * BLK // n_tgt
 
     slot_ids = jnp.arange(cap, dtype=jnp.int32)
-    combo = jnp.where(slot_ids < pair_counts[0], pair_blocks[:, 0] * tb + pair_blocks[:, 1], -1)
+    combo = pair_blocks[:, 0] * tb + pair_blocks[:, 1]
+    codes = combo + jnp.where(slot_ids < pair_counts[0], 0, sb * tb)
     combos = jnp.arange(sb * tb, dtype=jnp.int32)
-    slots = jnp.min(jnp.where(combo[None, :] == combos[:, None], slot_ids[None, :], cap), axis=1)
+    slots = jnp.min(jnp.where(codes[None, :] == combos[:, None], slot_ids[None, :], cap), axis=1)
 
     f32, bf16 = jnp.float32, jnp.bfloat16
     dma = pltpu.SemaphoreType.DMA
@@ -391,9 +427,13 @@
             jax.ShapeDtypeStruct((src_own, width), f32),
             jax.ShapeDtypeStruct((tgt_own, width), f32),
         ),
-        in_specs=[smem] * 3 + [vmem] * 4,
+        in_specs=[smem] * 2 + [pl.BlockSpec(memory_space=pltpu.HBM)] * 2 + [vmem] * 2,
         out_specs=(vmem, vmem),
         scratch_shapes=[
+            pltpu.VMEM((sb, BLK, width), bf16),
+            pltpu.VMEM((tb, BLK, width), bf16),
+            pltpu.VMEM((sb, BLK), f32),
+            pltpu.VMEM((tb, BLK), f32),
             pltpu.VMEM((cap, BLK, BLK), f32),
             pltpu.VMEM((cap, BLK, BLK), f32),
             pltpu.VMEM((cap + 1, BLK, BLK), bf16),
@@ -418,24 +458,24 @@
             dma((ITERS + 1, n_tgt)),
             dma((ITERS + 1, n_src)),
             dma((ITERS + 1, n_src)),
-            dma((n_outer,)),
-            dma((n_outer,)),
-            dma((n_outer,)),
-            dma((n_outer,)),
+            dma((n_outer, 2)),
+            dma((n_outer, 2)),
+            dma((n_outer, 2)),
+            dma((n_outer, 2)),
             dma((n_tgt,)),
             dma((n_tgt,)),
+            dma((2,)),
         ],
         compiler_params=pltpu.CompilerParams(
             collective_id=0, has_side_effects=True, vmem_limit_bytes=50 * 1024 * 1024
         ),
     )(
-        pair_blocks,
-        pair_counts,
+        codes,
         slots,
         text_emb.reshape(sb, BLK, width),
         image_emb.reshape(tb, BLK, width),
-        log_mass_src.reshape(sb, BLK),
-        log_mass_tgt.reshape(tb, BLK),
+        log_mass_src.reshape(-1, LANES),
+        log_mass_tgt.reshape(-1, LANES),
     )
 
 

time: 113 us -> 108 us (0.956)
  Pallas kernels: 105 us -> 101 us
    pallas_call x1, Pallas kernels: 105 us -> 101 us  [local(): pl.pallas_call(functools.partial(kernel, n_src, n_tgt, inner), out_shape=...]
    reshape x2 -> x0, local copies, waits for them, and re-layouts: 1.4 us -> none  [the longest x1 0.7 us: local(): log_mass_src.reshape(sb, BLK)]
    unnamed x5 -> x8, local copies, waits for them, and re-layouts: 4.11 us -> 4.74 us
where the time goes in v2:
time: 108 us; the launch traced here: 107 us
  Pallas kernels  101 us (94%)
  local copies, waits for them, and re-layouts  4.74 us (4%)
  between operations  1.3 us (1%)
    pallas_call x1, Pallas kernels, local(): pl.pallas_call(functools.partial(kernel, n_src, n_tgt, inner), out_shape=...  101 us
    unnamed x8, local copies, waits for them, and re-layouts  4.74 us

profile of v2, /device:TPU:0, one launch (start us, length us, event | category | flops | bytes accessed | tf_op | source)
XLA Modules:
  0.0 107.4 jit_solution(16314598344264964337)
XLA Ops:
  1.3 0.8 fusion.codes
  2.0 0.1 select_reduce_fusion.slots
  2.1 0.0 copy-start
  2.1 1.6 %copy-done = bf16[2048,512]{1,0:T(8,128)(2,1)S(1)} copy-done((bf16[2048,512]{1,0:T(8,128)(2,1)S(1)}, bf16[2048,512]{1,0:T(8,128)(2,1)}, u32[]{:S(2)}) %copy-start) | copy-done | bytes 2097176
  3.7 0.0 copy-start.1
  3.7 0.7 copy-done.1
  4.4 0.0 copy-start.2
  4.4 0.7 copy-done.2
  5.1 100.5 %shard_map.77 = (f32[512,512]{1,0:T(8,128)S(1)}, f32[256,512]{1,0:T(8,128)S(1)}) custom-call(s32[16]{0:T(128)S(1)} %fusion.codes, s32[64]{0:T(128)S(1)} %select_reduce_fusion.slots, bf16[8,256,512]{2,1,0:T(8,128)(2,1)S(1)} %bitcast.8, bf16[8,256,512]{2,1,0:T(8,128)(2,1)} %bitcast.11, f32[16,128]{1,0:T(8,128)S(1)} %bitcast.9, f32[16,128]{1,0:T(8,128)S(1)} %bitcast.10), custom_call_target="tpu_custom_call" | custom-call | tf_op jit(solution)/shard_map/pallas_call | solution.py:424
  105.7 1.0 copy.11
  106.6 0.8 copy.12
Async XLA Ops:
  2.1 1.6 %copy-start = (bf16[2048,512]{1,0:T(8,128)(2,1)S(1)}, bf16[2048,512]{1,0:T(8,128)(2,1)}, u32[]{:S(2)}) copy-start(bf16[2048,512]{1,0:T(8,128)(2,1)} %param.6) | copy-start | bytes 6291460
  3.7 0.7 copy-start.1
  4.4 0.7 copy-start.2

commit v3 on v2

--- a/solution.py
+++ b/solution.py
@@ -52,9 +52,9 @@
 
 def kernel(
     n_src, n_tgt, inner,
-    codes, slots, text_hbm, image_hbm, lines_src, lines_tgt,
+    codes, slots, text_hbm, image_hbm, lines_src_hbm, lines_tgt_hbm,
     src_out, tgt_out,
-    text, image, mass_src, mass_tgt,
+    text, image, lines_src, lines_tgt, mass_src, mass_tgt,
     score, score_t, weight, weight_t, bias_src, bias_tgt,
     src_wide, tgt_wide, src_row, tgt_row, top, tot,
     src_parts, tgt_parts,
@@ -77,6 +77,8 @@
     loads = [
         pltpu.make_async_copy(text_hbm, text, load_sem.at[0]),
         pltpu.make_async_copy(image_hbm, image, load_sem.at[1]),
+        pltpu.make_async_copy(lines_src_hbm, lines_src, load_sem.at[2]),
+        pltpu.make_async_copy(lines_tgt_hbm, lines_tgt, load_sem.at[3]),
     ]
     for load in loads:
         load.start()
@@ -99,22 +101,31 @@
         b = jnp.where(used, tgt_of(k), -1)
         bias_tgt[k] = jnp.where(cols == b, 0.0, floor_value)
 
+    def add_up(k, h, shifted):
+        lanes = pl.ds(h * LANES, LANES)
+        shifted = shifted.reshape(block // 8, 8, LANES)
+        peak = jnp.max(shifted, axis=0)
+        top[k, :, lanes] = peak
+        tot[k, :, lanes] = jnp.sum(jnp.exp(shifted - peak[None]), axis=0)
+
     def make_scores(k):
         rows, cols = text[src_of(k)], image[tgt_of(k)]
         nt = (((1,), (1,)), ((), ()))
         score[k] = lax.dot_general(rows, cols, nt, preferred_element_type=jnp.float32) * inv_temp
-        score_t[k] = lax.dot_general(cols, rows, nt, preferred_element_type=jnp.float32) * inv_temp
+        tile = lax.dot_general(cols, rows, nt, preferred_element_type=jnp.float32) * inv_temp
+        score_t[k] = tile
+        for h in range(block // LANES):
+            add_up(k, h, tile[:, h * LANES : (h + 1) * LANES])
 
     looped(0, cap, make_bias)
+    for load in loads:
+        load.wait()
     for lines, mass in ((lines_src, mass_src), (lines_tgt, mass_tgt)):
         for c in range(mass.shape[0]):
             for h in range(block // LANES):
                 line = c * (block // LANES) + h
                 mass[c : c + 1, h * LANES : (h + 1) * LANES] = lines[line : line + 1, :]
-    for load in loads:
-        load.wait()
     looped(0, cap, make_scores, unroll=2)
-    tgt_wide[...] = jnp.zeros_like(tgt_wide)
     pl.semaphore_wait(barrier, n_tgt - 1 + n_src - 1)
 
     def push(parts, step, me, n, device, ss, rs, d):
@@ -164,10 +175,7 @@
             shift = wide[cluster_of(k)]
             for h in range(block // LANES):
                 lanes = pl.ds(h * LANES, LANES)
-                shifted = (tiles[k, :, lanes] + shift).reshape(block // 8, 8, LANES)
-                peak = jnp.max(shifted, axis=0)
-                top[k, :, lanes] = peak
-                tot[k, :, lanes] = jnp.sum(jnp.exp(shifted - peak[None]), axis=0)
+                add_up(k, h, tiles[k, :, lanes] + shift)
 
         looped(0, cap, one, unroll=4)
 
@@ -194,7 +202,7 @@
             row[c] = value[c : c + 1, :]
 
     def iterate(step):
-        lse_pass(score_t, tgt_wide, tgt_of)
+        pl.when(step > 0)(lambda: lse_pass(score_t, tgt_wide, tgt_of))
         src_parts[step, t] = local_part(bias_src)
         send_parts("src", step)
         wait_parts("src", step)
@@ -211,31 +219,25 @@
 
     looped(0, ITERS, iterate)
 
-    def plan(k):
+    def plan_tgt(k):
         a, b = src_of(k), tgt_of(k)
         for h in range(block // LANES):
             lanes = pl.ds(h * LANES, LANES)
-            tile = score[k, :, lanes] + src_wide[a] + tgt_row[b, :, lanes]
-            tile = jnp.exp(tile)
+            tile = jnp.exp(score_t[k, :, lanes] + src_row[a, :, lanes] + tgt_wide[b])
+            weight_t[k, :, lanes] = tile.astype(jnp.bfloat16)
+            tot[k, :, lanes] = jnp.sum(tile.reshape(block // 8, 8, LANES), axis=0)
+
+    def plan_src(k):
+        a, b = src_of(k), tgt_of(k)
+        for h in range(block // LANES):
+            lanes = pl.ds(h * LANES, LANES)
+            tile = jnp.exp(score[k, :, lanes] + src_wide[a] + tgt_row[b, :, lanes])
             weight[k, :, lanes] = tile.astype(jnp.bfloat16)
             top[k, :, lanes] = jnp.sum(tile.reshape(block // 8, 8, LANES), axis=0)
-            tile = score_t[k, :, lanes] + src_row[a, :, lanes] + tgt_wide[b]
-            tile = jnp.exp(tile)
-            weight_t[k, :, lanes] = tile.astype(jnp.bfloat16)
-            tot[k, :, lanes] = jnp.sum(tile.reshape(block // 8, 8, LANES), axis=0)
-
-    looped(0, cap, plan, unroll=2)
-    weight[cap] = jnp.zeros(weight.shape[1:], weight.dtype)
-    weight_t[cap] = jnp.zeros(weight_t.shape[1:], weight_t.dtype)
 
     def mass_part(sums, bias):
         rows = jnp.sum(sums[...], axis=1, keepdims=True)
         return jnp.sum(jnp.where(bias[...] == 0.0, rows, 0.0), axis=0)
-
-    src_parts[ITERS, t] = mass_part(tot, bias_src)
-    tgt_parts[ITERS, s] = mass_part(top, bias_tgt)
-    send_parts("tgt", ITERS)
-    send_parts("src", ITERS)
 
     def unit_rows(n, clusters):
         own = clusters * block // n
@@ -331,8 +333,16 @@
         z = partner(outer, n_outer, step)
         tgt_numer(z * inner + side, outer_sum, z)
 
+    looped(0, cap, plan_tgt, unroll=2)
+    weight_t[cap] = jnp.zeros(weight_t.shape[1:], weight_t.dtype)
     if inner == 2:
         looped(0, n_outer, to_mate)
+    looped(0, cap, plan_src, unroll=2)
+    weight[cap] = jnp.zeros(weight.shape[1:], weight.dtype)
+    src_parts[ITERS, t] = mass_part(tot, bias_src)
+    tgt_parts[ITERS, s] = mass_part(top, bias_tgt)
+    send_parts("tgt", ITERS)
+    send_parts("src", ITERS)
     looped(0, n_tgt - 1, to_part)
     looped(0, n_outer, own_outer)
 
@@ -427,11 +437,13 @@
             jax.ShapeDtypeStruct((src_own, width), f32),
             jax.ShapeDtypeStruct((tgt_own, width), f32),
         ),
-        in_specs=[smem] * 2 + [pl.BlockSpec(memory_space=pltpu.HBM)] * 2 + [vmem] * 2,
+        in_specs=[smem] * 2 + [pl.BlockSpec(memory_space=pltpu.HBM)] * 4,
         out_specs=(vmem, vmem),
         scratch_shapes=[
             pltpu.VMEM((sb, BLK, width), bf16),
             pltpu.VMEM((tb, BLK, width), bf16),
+            pltpu.VMEM((sb * BLK // LANES, LANES), f32),
+            pltpu.VMEM((tb * BLK // LANES, LANES), f32),
             pltpu.VMEM((sb, BLK), f32),
             pltpu.VMEM((tb, BLK), f32),
             pltpu.VMEM((cap, BLK, BLK), f32),
@@ -464,10 +476,10 @@
             dma((n_outer, 2)),
             dma((n_tgt,)),
             dma((n_tgt,)),
-            dma((2,)),
+            dma((4,)),
         ],
         compiler_params=pltpu.CompilerParams(
-            collective_id=0, has_side_effects=True, vmem_limit_bytes=50 * 1024 * 1024
+            collective_id=0, has_side_effects=True, vmem_limit_bytes=56 * 1024 * 1024
         ),
     )(
         codes,

time: 108 us -> 108 us (level)
  local copies, waits for them, and re-layouts: 4.74 us -> 3.12 us
    unnamed x8 -> x6, local copies, waits for them, and re-layouts: 4.74 us -> 3.12 us
    pallas_call x1, Pallas kernels: 101 us -> 102 us  [local(): pl.pallas_call(functools.partial(kernel, n_src, n_tgt, inner), out_shape=...]
where the time goes in v3:
time: 108 us
  Pallas kernels  102 us (94%)
  local copies, waits for them, and re-layouts  3.12 us (3%)
  other arithmetic  1.36 us (1%)
  between operations  1.3 us (1%)
    pallas_call x1, Pallas kernels, local(): pl.pallas_call(functools.partial(kernel, n_src, n_tgt, inner), out_shape=...  102 us
    unnamed x6, local copies, waits for them, and re-layouts  3.12 us

profile of v3, /device:TPU:0, one launch (start us, length us, event | category | flops | bytes accessed | tf_op | source)
XLA Modules:
  0.0 107.8 jit_solution(9429871966622943101)
XLA Ops:
  1.3 0.8 fusion.codes
  2.0 0.0 copy-start.1
  2.0 0.6 select_reduce_fusion.slots
  2.6 0.0 copy-done.1
  2.6 102.0 %shard_map.77 = (f32[512,512]{1,0:T(8,128)}, f32[256,512]{1,0:T(8,128)}) custom-call(s32[16]{0:T(128)} %copy-done.1, s32[64]{0:T(128)} %select_reduce_fusion.slots, bf16[8,256,512]{2,1,0:T(8,128)(2,1)} %bitcast.8, bf16[8,256,512]{2,1,0:T(8,128)(2,1)} %bitcast.9, f32[16,128]{1,0:T(8,128)} %bitcast.10, f32[16,128]{1,0:T(8,128)} %bitcast.11), custom_call_target="tpu_custom_call" | custom-call | tf_op jit(solution)/shard_map/pallas_call | solution.py:434
  104.7 0.0 copy-start
  104.7 2.3 %copy.11 = f32[512,512]{1,0:T(8,128)} copy(f32[512,512]{1,0:T(8,128)} %get-tuple-element.4) | data formatting | bytes 2097152
  107.0 0.0 copy-done
  107.0 0.8 copy.12
Async XLA Ops:
  2.0 0.6 copy-start.1
  104.7 2.3 %copy-start = (f32[256,512]{1,0:T(8,128)S(1)}, f32[256,512]{1,0:T(8,128)}, u32[]{:S(2)}) copy-start(f32[256,512]{1,0:T(8,128)} %get-tuple-element.5) | copy-start | bytes 1572868

commit v4 on v3

--- a/solution.py
+++ b/solution.py
@@ -479,7 +479,7 @@
             dma((4,)),
         ],
         compiler_params=pltpu.CompilerParams(
-            collective_id=0, has_side_effects=True, vmem_limit_bytes=56 * 1024 * 1024
+            collective_id=0, has_side_effects=True, vmem_limit_bytes=53 * 1024 * 1024
         ),
     )(
         codes,

time: 108 us -> 109 us (level)
  local copies, waits for them, and re-layouts: 3.12 us -> 4.44 us
    unnamed x6, local copies, waits for them, and re-layouts: 3.12 us -> 4.44 us
where the time goes in v4:
time: 109 us; the launch traced here: 108 us
  Pallas kernels  102 us (94%)
  local copies, waits for them, and re-layouts  4.44 us (4%)
  between operations  1.29 us (1%)
    pallas_call x1, Pallas kernels, local(): pl.pallas_call(functools.partial(kernel, n_src, n_tgt, inner), out_shape=...  102 us
    unnamed x6, local copies, waits for them, and re-layouts  4.44 us

profile of v4, /device:TPU:0, one launch (start us, length us, event | category | flops | bytes accessed | tf_op | source)
XLA Modules:
  0.0 108.3 jit_solution(11657374834203882096)
XLA Ops:
  1.3 0.8 fusion.codes
  2.0 0.1 select_reduce_fusion.slots
  2.1 0.0 copy-start
  2.1 0.7 copy-done
  2.8 0.0 copy-start.1
  2.8 0.7 copy-done.1
  3.5 101.7 %shard_map.77 = (f32[512,512]{1,0:T(8,128)}, f32[256,512]{1,0:T(8,128)S(1)}) custom-call(s32[16]{0:T(128)S(1)} %fusion.codes, s32[64]{0:T(128)S(1)} %select_reduce_fusion.slots, bf16[8,256,512]{2,1,0:T(8,128)(2,1)} %bitcast.10, bf16[8,256,512]{2,1,0:T(8,128)(2,1)} %bitcast.11, f32[16,128]{1,0:T(8,128)S(1)} %bitcast.8, f32[16,128]{1,0:T(8,128)S(1)} %bitcast.9), custom_call_target="tpu_custom_call" | custom-call | tf_op jit(solution)/shard_map/pallas_call | solution.py:434
  105.3 2.3 %copy.11 = f32[512,512]{1,0:T(8,128)} copy(f32[512,512]{1,0:T(8,128)} %get-tuple-element.4) | data formatting | bytes 2097152
  107.5 0.8 copy.12
Async XLA Ops:
  2.1 0.7 copy-start
  2.8 0.7 copy-start.1
